TPU v7x, 128 devices: a whole 4x4x4 slice. The times are simulated.
128 devices in a mesh: wide: 16 (over x_hi, z, core), node: 8 (over x_lo, y).
Axes of the slice: x: 4 (x_hi: 2, x_lo: 2; x = x_hi * 2 + x_lo), y: 4, z: 4, core: 2. Of those that a mesh axis runs over, the one named last changes fastest.
Arguments:
- tokens: bfloat16 [12288, 3072], P('wide', 'node'), may hold values from -6 to 6
- target: bfloat16 [12288, 3072], P('wide', 'node'), may hold values from -6 to 6
- mod_table: bfloat16 [32, 3072], P(None, 'node'), may hold values from -1.5 to 1.5
- adv_table: float32 [32, 16], replicated, may hold values from 0.25 to 4
- w_up: bfloat16 [3072, 7168], P('wide', 'node'), may hold values from -0.109375 to 0.109375
- w_down_t: bfloat16 [3072, 7168], P('wide', 'node'), may hold values from -0.0625 to 0.0625
- bins: int32 [48], P('wide'), may hold values from 0 to 31
- groups: int32 [48], P('wide'), may hold values from 0 to 15
Outputs:
- grad_tokens: float32 [12288, 3072], P('wide', 'node')
- grad_up: float32 [3072, 7168], P('wide', 'node')
- grad_down: float32 [3072, 7168], P('wide', 'node')
All inputs are finite; a program needn't handle non-finite values.
Results may differ from a plain program's by a relative error of at most 0.02.
Values may be sent and summed in bfloat16 or wider, within the bound.
A program may use at most 128 MiB of HBM per device.

v0:
```python
import jax
import jax.numpy as jnp
from jax import lax
from jax.sharding import PartitionSpec as P


def gelu_tanh(value):
    return jax.nn.gelu(value, approximate=True)


def contract_last(left, right):
    return lax.dot_general(
        left, right, (((1,), (1,)), ((), ())), preferred_element_type=jnp.float32
    )


def on_device(tokens, target, mod_table, adv_table, w_up, w_down_t, bins, groups):
    full_tok, full_mod = (
        lax.all_gather(tokens, "node", axis=1, tiled=True),
        lax.all_gather(mod_table, "node", axis=1, tiled=True),
    )
    rows = tokens.shape[0]
    micro = bins.shape[0]
    seq = rows // micro
    width = full_tok.shape[1]
    local_width = tokens.shape[1]
    bin_hot = (bins[:, None] == jnp.arange(adv_table.shape[0])[None, :]).astype(jnp.float32)
    grp_hot = (groups[:, None] == jnp.arange(adv_table.shape[1])[None, :]).astype(jnp.float32)
    high = lax.Precision.HIGHEST
    gain_full = 1.0 + jnp.dot(bin_hot, full_mod.astype(jnp.float32), precision=high)
    gain_local = 1.0 + jnp.dot(bin_hot, mod_table.astype(jnp.float32), precision=high)
    weight = jnp.sum(jnp.dot(bin_hot, adv_table, precision=high) * grp_hot, axis=1)
    modulated = (
        (full_tok.reshape(micro, seq, width).astype(jnp.float32) * gain_full[:, None, :])
        .astype(jnp.bfloat16)
        .reshape(rows, width)
    )
    hidden_cols = w_up.shape[1]

    def fold_rows(left, piece):
        return jnp.dot(left, piece, preferred_element_type=jnp.float32)

    def map_rows(left, piece):
        return contract_last(left, piece)

    pre = fold_rows(modulated, lax.all_gather(w_up, "wide", axis=0, tiled=True))
    hidden = gelu_tanh(pre).astype(jnp.bfloat16)
    delta_part = map_rows(hidden, lax.all_gather(w_down_t, "wide", axis=0, tiled=True))
    delta = lax.psum_scatter(
        delta_part.astype(jnp.bfloat16), "node", scatter_dimension=1, tiled=True
    ).astype(jnp.float32)
    err = tokens.astype(jnp.float32) + delta - target.astype(jnp.float32)
    dpred = (err.reshape(micro, seq, local_width) * weight[:, None, None]).reshape(
        rows, local_width
    )
    dy = dpred.astype(jnp.bfloat16)
    dy_full = lax.all_gather(dy, "node", axis=1, tiled=True)
    pull = jax.vjp(gelu_tanh, pre)[1]
    dh = fold_rows(dy_full, lax.all_gather(w_down_t, "wide", axis=0, tiled=True))
    dpre = pull(dh)[0].astype(jnp.bfloat16)
    dmod_part = map_rows(dpre, lax.all_gather(w_up, "wide", axis=0, tiled=True))
    dmod = lax.psum_scatter(
        dmod_part.astype(jnp.bfloat16), "node", scatter_dimension=1, tiled=True
    ).astype(jnp.float32)
    grad_tokens = dpred + (gain_local[:, None, :] * dmod.reshape(micro, seq, local_width)).reshape(
        rows, local_width
    )
    scale = float(lax.axis_size("wide") * rows) ** (-0.5)
    term_up = lax.dot_general(
        modulated, dpre, (((0,), (0,)), ((), ())), preferred_element_type=jnp.float32
    )
    term_down = lax.dot_general(
        dy_full, hidden, (((0,), (0,)), ((), ())), preferred_element_type=jnp.float32
    )
    summed = lax.psum_scatter(
        (jnp.concatenate([term_up, term_down], axis=1) * scale).astype(jnp.bfloat16),
        "wide",
        scatter_dimension=0,
        tiled=True,
    ).astype(jnp.float32)
    grad_up = summed[:, :hidden_cols]
    grad_down = summed[:, hidden_cols:]
    return (grad_tokens, grad_up, grad_down)


def solution(mesh):
    return jax.shard_map(
        on_device,
        mesh=mesh,
        in_specs=(
            P("wide", "node"),
            P("wide", "node"),
            P(None, "node"),
            P(),
            P("wide", "node"),
            P("wide", "node"),
            P("wide"),
            P("wide"),
        ),
        out_specs=(P("wide", "node"), P("wide", "node"), P("wide", "node")),
        check_vma=False,
    )
```

profile of v0, /device:TPU:1, one launch (start us, length us, event | category | flops | bytes accessed | tf_op | source)
XLA Modules:
  0.0 538.0 jit_solution(9273582299312235300)
XLA Ops:
  7.2 0.0 copy-start
  7.2 0.0 all-gather.5.cloned.1.call-start
  7.2 0.7 all-gather.5.cloned.1.call-update
  7.9 0.0 all-gather.7.cloned.1.call-start
  8.0 0.7 all-gather.7.cloned.1.call-update
  8.7 0.0 all-gather.9.cloned.1.call-start
  8.7 0.7 all-gather.9.cloned.1.call-update
  9.4 0.0 reduce-scatter.10.cloned.1.call-start
  9.4 25.2 %all_gather.18 = bf16[32,3072]{1,0:T(8,128)(2,1)S(1)} all-gather(bf16[32,384]{1,0:T(8,128)(2,1)} %param.10), channel_id=1, replica_groups=mesh['wide'=16,'node'=8] {'node'}, dimensions={1}, use_global_device_ids=true | all-gather | bytes 221184 | tf_op jit(solution)/shard_map/all_gather | solution.py:20
  34.6 0.9 convolution_add_fusion
  35.5 36.5 %all-gather.5.cloned.1.call-done = bf16[768,3072]{1,0:T(8,128)(2,1)} async-done(((bf16[768,384]{1,0:T(8,128)(2,1)}), bf16[768,3072]{1,0:T(8,128)(2,1)}) %all-gather.5.cloned.1.call-update) | async-done | bytes 4718608 | tf_op jit(solution)/shard_map/all_gather | solution.py:19
  72.0 5.7 %fusion.1 = bf16[768,3072]{1,0:T(8,128)(2,1)} fusion(bf16[768,3072]{1,0:T(8,128)(2,1)} %all-gather.5.cloned.1.call-done, f32[3,3072]{1,0:T(4,128)S(1)} %convolution_add_fusion), kind=kLoop, calls=%fused_computation.3 | loop fusion | flops 7077888 | bytes 9474048 | tf_op jit(solution)/shard_map/convert_element_type | solution.py:35
  77.7 56.7 %all-gather.7.cloned.1.call-done = bf16[3072,896]{1,0:T(8,128)(2,1)} async-done(((bf16[192,896]{1,0:T(8,128)(2,1)}), bf16[3072,896]{1,0:T(8,128)(2,1)}) %all-gather.7.cloned.1.call-update) | async-done | bytes 5505040 | tf_op jit(solution)/shard_map/all_gather | solution.py:46
  134.3 8.5 %fusion.17 = f32[768,896]{1,0:T(8,128)S(1)} fusion(bf16[768,3072]{1,0:T(8,128)(2,1)} %fusion.1, bf16[3072,896]{1,0:T(8,128)(2,1)} %all-gather.7.cloned.1.call-done), kind=kOutput, calls=%fused_computation.31 | convolution fusion | flops 4227858432 | bytes 12976128 | tf_op jit(solution)/shard_map/dot_general | solution.py:41
  142.8 0.0 copy-start.7
  142.9 52.7 %all-gather.9.cloned.1.call-done = bf16[3072,896]{1,0:T(8,128)(2,1)} async-done(((bf16[192,896]{1,0:T(8,128)(2,1)}), bf16[3072,896]{1,0:T(8,128)(2,1)}) %all-gather.9.cloned.1.call-update) | async-done | bytes 5505040 | tf_op jit(solution)/shard_map/all_gather | solution.py:48
  195.6 9.4 %convolution_convert_fusion.1 = bf16[768,3072]{1,0:T(8,128)(2,1)} fusion(bf16[3072,896]{1,0:T(8,128)(2,1)} %all-gather.9.cloned.1.call-done, f32[768,896]{1,0:T(8,128)S(1)} %fusion.17), kind=kOutput, calls=%fused_computation.5 | convolution fusion | flops 4236410880 | bytes 12976128 | tf_op jit(solution)/shard_map/dot_general | solution.py:12
  205.0 0.0 copy-done.7
  205.0 6.6 %copy.15 = bf16[768,3072]{0,1:T(8,128)(2,1)} copy(bf16[768,3072]{1,0:T(8,128)(2,1)} %convolution_convert_fusion.1) | data formatting | bytes 9437184
  211.6 0.0 copy-start.5
  211.6 0.0 copy-start.6
  211.6 0.0 copy-start.3
  211.6 0.0 reduce-scatter.10.cloned.1.call-update
  211.6 0.0 all-gather.11.cloned.1.call-start
  211.7 0.0 copy-done
  211.7 0.6 copy-done.5
  212.3 0.0 copy-done.6
  212.3 0.3 fusion.10
  212.6 0.1 mul.99
  212.7 54.6 %reduce-scatter.10.cloned.1.call-done = bf16[384,768]{1,0:T(8,128)(2,1)} async-done(((bf16[3072,768]{1,0:T(8,128)(2,1)}), bf16[384,768]{1,0:T(8,128)(2,1)}) %reduce-scatter.10.cloned.1.call-update) | async-done | bytes 589840
  267.2 1.4 copy.16
  268.6 0.0 copy-done.2
  268.6 0.0 copy-done.3
  268.6 1.1 fusion.11
  269.7 0.0 all-gather.11.cloned.1.call-update
  269.7 0.0 reduce-scatter.12.cloned.1.call-start
  269.8 56.4 %all-gather.11.cloned.1.call-done = bf16[768,3072]{1,0:T(8,128)(2,1)} async-done(((bf16[768,384]{1,0:T(8,128)(2,1)}), bf16[768,3072]{1,0:T(8,128)(2,1)}) %all-gather.11.cloned.1.call-update) | async-done | bytes 4718608 | tf_op jit(solution)/shard_map/all_gather | solution.py:57
  326.1 10.0 %fusion.8 = bf16[768,896]{1,0:T(8,128)(2,1)S(1)} fusion(f32[768,896]{1,0:T(8,128)} %copy-done.7, bf16[768,3072]{1,0:T(8,128)(2,1)} %all-gather.11.cloned.1.call-done, bf16[3072,896]{1,0:T(8,128)(2,1)} %all-gather.9.cloned.1.call-done), kind=kOutput, calls=%fused_computation.15 | convolution fusion | flops 4241620992 | bytes 14352384 | tf_op jit(solution)/shard_map/dot_general | solution.py:41
  336.1 0.0 copy-start.9
  336.1 1.1 copy-done.9
  337.2 9.3 %convolution_convert_fusion = bf16[768,3072]{1,0:T(8,128)(2,1)} fusion(bf16[768,896]{1,0:T(8,128)(2,1)S(1)} %fusion.8, bf16[3072,896]{1,0:T(8,128)(2,1)} %all-gather.7.cloned.1.call-done), kind=kOutput, calls=%fused_computation.4 | convolution fusion | flops 4230217728 | bytes 11599872 | tf_op jit(solution)/shard_map/dot_general | solution.py:12
  346.5 6.6 %copy.17 = bf16[768,3072]{0,1:T(8,128)(2,1)} copy(bf16[768,3072]{1,0:T(8,128)(2,1)} %convolution_convert_fusion) | data formatting | bytes 9437184
  353.1 0.0 reduce-scatter.12.cloned.1.call-update
  353.1 0.2 reduce-scatter.14.cloned.1.call-start
  353.4 0.0 copy-start.8
  353.4 6.9 %fusion.18 = f32[3072,896]{0,1:T(8,128)S(1)} fusion(bf16[768,3072]{1,0:T(8,128)(2,1)} %fusion.1, bf16[768,896]{1,0:T(8,128)(2,1)} %copy-done.9), kind=kOutput, calls=%fused_computation.32 | convolution fusion | flops 4227858432 | bytes 17104896 | tf_op jit(solution)/shard_map/dot_general | solution.py:69
  360.3 0.0 copy-done.8
  360.3 7.1 %fusion.15 = f32[3072,896]{0,1:T(8,128)S(1)} fusion(bf16[768,3072]{1,0:T(8,128)(2,1)} %all-gather.11.cloned.1.call-done, f32[768,896]{1,0:T(8,128)S(1)} %copy-done.8), kind=kOutput, calls=%fused_computation.29 | convolution fusion | flops 4234051584 | bytes 18481152 | tf_op jit(solution)/shard_map/dot_general | solution.py:72
  367.4 6.3 %fusion = bf16[3072,1792]{0,1:T(8,128)(2,1)} fusion(f32[3072,896]{0,1:T(8,128)S(1)} %fusion.15, f32[3072,896]{0,1:T(8,128)S(1)} %fusion.18), kind=kLoop, calls=%fused_computation.1 | loop fusion | flops 16515072 | bytes 33030144 | tf_op jit(solution)/shard_map/convert_element_type | solution.py:76
  373.8 14.3 %copy.19 = bf16[3072,1792]{1,0:T(8,128)(2,1)} copy(bf16[3072,1792]{0,1:T(8,128)(2,1)} %fusion) | data formatting | bytes 22020096
  388.1 0.0 copy-start.4
  388.1 0.0 reduce-scatter.14.cloned.1.call-update
  388.1 0.7 copy-done.4
  388.8 0.2 convolution_add_fusion.1
  389.0 21.1 %reduce-scatter.12.cloned.1.call-done = bf16[384,768]{1,0:T(8,128)(2,1)} async-done(((bf16[3072,768]{1,0:T(8,128)(2,1)}), bf16[384,768]{1,0:T(8,128)(2,1)}) %reduce-scatter.12.cloned.1.call-update) | async-done | bytes 589840
  410.1 1.4 copy.18
  411.5 1.4 fusion.9
  412.9 114.4 %reduce-scatter.14.cloned.1.call-done = bf16[192,1792]{1,0:T(8,128)(2,1)} async-done(((bf16[3072,1792]{1,0:T(8,128)(2,1)}), bf16[192,1792]{1,0:T(8,128)(2,1)}) %reduce-scatter.14.cloned.1.call-update) | async-done | bytes 688144
  527.3 0.0 copy-start.1
  527.3 1.4 copy.20
  528.7 0.1 fusion.16
  528.9 1.1 copy.14
  530.0 1.1 copy.13
  531.1 0.0 copy-done.1
  (2 shorter events, 0.0 us)
Async XLA Ops:
  7.2 204.5 %copy-start = (f32[32,16]{0,1:T(8,128)S(1)}, f32[32,16]{0,1:T(8,128)}, u32[]{:S(2)}) copy-start(f32[32,16]{0,1:T(8,128)} %param.11) | copy-start | bytes 6148
  7.2 64.8 %all-gather.5.cloned.1.call-start = ((), (), s32[]{:S(2)}) async-start(), calls=%async_computation.3 | async-start | bytes 5308416 | tf_op jit(solution)/shard_map/all_gather | solution.py:19
  7.9 126.4 %all-gather.7.cloned.1.call-start = ((), (), s32[]{:S(2)}) async-start(), calls=%async_computation.4 | async-start | bytes 5849088 | tf_op jit(solution)/shard_map/all_gather | solution.py:46
  8.7 186.9 %all-gather.9.cloned.1.call-start = ((), (), s32[]{:S(2)}) async-start(), calls=%async_computation.5 | async-start | bytes 5849088 | tf_op jit(solution)/shard_map/all_gather | solution.py:48
  9.4 257.8 %reduce-scatter.10.cloned.1.call-start = ((), (), s32[]{:S(2)}) async-start(), calls=%async_computation.7 | async-start | bytes 5308416
  142.8 62.1 %copy-start.7 = (f32[768,896]{1,0:T(8,128)}, f32[768,896]{1,0:T(8,128)S(1)}, u32[]{:S(2)}) copy-start(f32[768,896]{1,0:T(8,128)S(1)} %fusion.17) | copy-start | bytes 8257540
  211.6 0.7 copy-start.5
  211.6 0.7 copy-start.6
  211.6 57.0 %copy-start.2 = (bf16[768,384]{1,0:T(8,128)(2,1)S(1)}, bf16[768,384]{1,0:T(8,128)(2,1)}, u32[]{:S(2)}) copy-start(bf16[768,384]{1,0:T(8,128)(2,1)} %param.8) | copy-start | bytes 1769476
  211.6 57.0 %copy-start.3 = (bf16[768,384]{1,0:T(8,128)(2,1)S(1)}, bf16[768,384]{1,0:T(8,128)(2,1)}, u32[]{:S(2)}) copy-start(bf16[768,384]{1,0:T(8,128)(2,1)} %param.9) | copy-start | bytes 1769476
  211.6 114.5 %all-gather.11.cloned.1.call-start = ((), (), s32[]{:S(2)}) async-start(), calls=%async_computation.6 | async-start | bytes 5308416 | tf_op jit(solution)/shard_map/all_gather | solution.py:57
  269.7 140.4 %reduce-scatter.12.cloned.1.call-start = ((), (), s32[]{:S(2)}) async-start(), calls=%async_computation.8 | async-start | bytes 5308416
  336.1 1.1 copy-start.9
  353.1 174.1 %reduce-scatter.14.cloned.1.call-start = ((), (), s32[]{:S(2)}) async-start(), calls=%async_computation.9 | async-start | bytes 11698176
  353.4 7.0 %copy-start.8 = (f32[768,896]{1,0:T(8,128)S(1)}, f32[768,896]{1,0:T(8,128)}, u32[]{:S(2)}) copy-start(f32[768,896]{1,0:T(8,128)} %copy-done.7) | copy-start | bytes 8257540
  388.1 0.7 copy-start.4
  527.3 3.9 copy-start.1
Sparse Core Ops, SparseCore 0:
  9.7 62.2 all-gather.4
  74.4 59.8 all-gather.6
  136.8 58.7 all-gather.8
  211.8 55.4 reduce-scatter.9
  269.8 56.2 all-gather.10
  353.3 56.8 reduce-scatter.11
  414.5 112.7 reduce-scatter.13
where the time goes:
time: 539 us; the launch traced here: 538 us
  waiting for transfers between devices  394 us (73%)
  matrix products  52.5 us (10%)
  local copies, waits for them, and re-layouts  36.6 us (7%)
  blocking collectives  25.2 us (5%)
  other arithmetic  14.5 us (3%)
  between operations  14.3 us (3%)
    unnamed x10, waiting for transfers between devices  192 us
    all_gather x1, waiting for transfers between devices, on_device(): pre = fold_rows(modulated, lax.all_gather(w_up, 'wide', axis=0, tiled=True))  56.7 us
    all_gather x1, waiting for transfers between devices, on_device(): dy_full = lax.all_gather(dy, 'node', axis=1, tiled=True)  56.4 us
    all_gather x1, waiting for transfers between devices, on_device(): lax.all_gather(w_down_t, 'wide', axis=0, tiled=True)  52.7 us
    all_gather x1, waiting for transfers between devices, on_device(): lax.all_gather(tokens, 'node', axis=1, tiled=True)  36.5 us
    unnamed x28, local copies, waits for them, and re-layouts  36.4 us
    all_gather x1, blocking collectives, on_device(): lax.all_gather(mod_table, 'node', axis=1, tiled=True)  25.2 us
    dot_general x2, matrix products, contract_last(): lax.dot_general(left, right, (((1,), (1,)), ((), ())), preferred_element_...  18.7 us
  transfers between devices with their start and end apart: 7, of which 7 were waited for; matrix products, arithmetic and copies ran while one was open for 10% of the time, Pallas kernels for 0%

commit v1 on v0

--- a/solution.py
+++ b/solution.py
@@ -45,7 +45,12 @@
 
     pre = fold_rows(modulated, lax.all_gather(w_up, "wide", axis=0, tiled=True))
     hidden = gelu_tanh(pre).astype(jnp.bfloat16)
-    delta_part = map_rows(hidden, lax.all_gather(w_down_t, "wide", axis=0, tiled=True))
+    delta_part = map_rows(
+        hidden,
+        jnp.concatenate(
+            lax.all_to_all(jnp.stack([w_down_t] * lax.axis_size("wide")), "wide", 0, 0), axis=0
+        ),
+    )
     delta = lax.psum_scatter(
         delta_part.astype(jnp.bfloat16), "node", scatter_dimension=1, tiled=True
     ).astype(jnp.float32)

time: 539 us -> 598 us (1.11)
  blocking collectives: 25.2 us -> 132 us
  waiting for transfers between devices: 394 us -> 333 us
  starting transfers between devices: 0.46 us -> 9.88 us
    all_gather x1, blocking collectives: 25.2 us -> 132 us  [on_device(): lax.all_gather(mod_table, 'node', axis=1, tiled=True)]
    all_gather x1, waiting for transfers between devices: 36.5 us -> 0.02 us  [on_device(): lax.all_gather(tokens, 'node', axis=1, tiled=True)]
    all_gather x1, waiting for transfers between devices: 56.7 us -> 23 us  [on_device(): pre = fold_rows(modulated, lax.all_gather(w_up, 'wide', axis=0, tiled=True))]
    all_to_all x0 -> x1, starting transfers between devices: none -> 9.42 us  [on_device(): lax.all_to_all(jnp.stack([w_down_t] * lax.axis_size('wide')), 'wide', 0, 0)]
    all_gather x1, waiting for transfers between devices: 52.7 us -> 60 us  [on_device(): lax.all_gather(w_down_t, 'wide', axis=0, tiled=True)]
    unnamed x28 -> x26, local copies, waits for them, and re-layouts: 36.4 us -> 34.9 us
  transfers between devices with their start and end apart: 7 -> 8, of which waited for: 7 -> 6; matrix products, arithmetic and copies ran while one was open for 10% -> 10% of each run, Pallas kernels for 0% -> 0%
where the time goes in v1:
time: 598 us; the launch traced here: 597 us
  waiting for transfers between devices  333 us (56%)
  blocking collectives  132 us (22%)
  matrix products  53.2 us (9%)
  local copies, waits for them, and re-layouts  39.2 us (7%)
  other arithmetic  15.1 us (3%)
  between operations  14.3 us (2%)
  starting transfers between devices  9.88 us (2%)
    unnamed x10, waiting for transfers between devices  193 us
    all_gather x1, blocking collectives, on_device(): lax.all_gather(mod_table, 'node', axis=1, tiled=True)  132 us
    all_gather x1, waiting for transfers between devices, on_device(): lax.all_gather(w_down_t, 'wide', axis=0, tiled=True)  60 us
    all_gather x1, waiting for transfers between devices, on_device(): dy_full = lax.all_gather(dy, 'node', axis=1, tiled=True)  56.9 us
    unnamed x26, local copies, waits for them, and re-layouts  34.9 us
    all_gather x1, waiting for transfers between devices, on_device(): pre = fold_rows(modulated, lax.all_gather(w_up, 'wide', axis=0, tiled=True))  23 us
    dot_general x2, matrix products, fold_rows(): return jnp.dot(left, piece, preferred_element_type=jnp.float32)  19.6 us
    dot_general x2, matrix products, contract_last(): lax.dot_general(left, right, (((1,), (1,)), ((), ())), preferred_element_...  18.9 us
  transfers between devices with their start and end apart: 8, of which 6 were waited for; matrix products, arithmetic and copies ran while one was open for 10% of the time, Pallas kernels for 0%

profile of v1, /device:TPU:1, one launch (start us, length us, event | category | flops | bytes accessed | tf_op | source)
XLA Modules:
  0.0 597.1 jit_solution(16226407181715458351)
XLA Ops:
  7.2 0.0 copy-start
  7.2 0.0 all-gather.5.cloned.1.call-start
  7.2 0.7 all-gather.5.cloned.1.call-update
  7.9 0.0 all-gather.7.cloned.1.call-start
  8.0 0.7 all-gather.7.cloned.1.call-update
  8.7 4.1 stack.2
  12.8 0.0 copy-start.4
  12.8 0.0 copy-start.5
  12.8 9.4 %all-to-all-start = ((bf16[16,192,896]{2,1,0:T(8,128)(2,1)}), bf16[16,192,896]{2,1,0:T(8,128)(2,1)}, u32[]{:S(2)}, u32[]{:S(2)}) async-start(bf16[16,192,896]{2,1,0:T(8,128)(2,1)} %stack.2), calls=%async_computation | async-start | bytes 11010048 | tf_op jit(solution)/shard_map/all_to_all | solution.py:51
  22.2 0.0 reduce-scatter.10.cloned.1.call-start
  22.2 0.0 copy-done.4
  22.2 132.4 %all_gather.17 = bf16[32,3072]{1,0:T(8,128)(2,1)S(1)} all-gather(bf16[32,384]{1,0:T(8,128)(2,1)S(1)} %copy-done.4), channel_id=1, replica_groups=mesh['wide'=16,'node'=8] {'node'}, dimensions={1}, use_global_device_ids=true | all-gather | bytes 221184 | tf_op jit(solution)/shard_map/all_gather | solution.py:20
  154.6 0.0 copy-done.5
  154.6 0.2 convolution_add_fusion
  154.8 0.0 all-gather.5.cloned.1.call-done
  154.8 6.4 %fusion.1 = bf16[768,3072]{1,0:T(8,128)(2,1)} fusion(bf16[768,3072]{1,0:T(8,128)(2,1)} %all-gather.5.cloned.1.call-done, f32[3,3072]{1,0:T(4,128)S(1)} %convolution_add_fusion), kind=kLoop, calls=%fused_computation.3 | loop fusion | flops 7077888 | bytes 9474048 | tf_op jit(solution)/shard_map/convert_element_type | solution.py:35
  161.2 23.0 %all-gather.7.cloned.1.call-done = bf16[3072,896]{1,0:T(8,128)(2,1)} async-done(((bf16[192,896]{1,0:T(8,128)(2,1)}), bf16[3072,896]{1,0:T(8,128)(2,1)}) %all-gather.7.cloned.1.call-update) | async-done | bytes 5505040 | tf_op jit(solution)/shard_map/all_gather | solution.py:46
  184.2 9.6 %fusion.17 = f32[768,896]{1,0:T(8,128)} fusion(bf16[768,3072]{1,0:T(8,128)(2,1)} %fusion.1, bf16[3072,896]{1,0:T(8,128)(2,1)} %all-gather.7.cloned.1.call-done), kind=kOutput, calls=%fused_computation.31 | convolution fusion | flops 4227858432 | bytes 12976128 | tf_op jit(solution)/shard_map/dot_general | solution.py:41
  193.8 0.0 all-to-all-done
  193.8 9.6 %convolution_convert_fusion.1 = bf16[768,3072]{1,0:T(8,128)(2,1)} fusion(bf16[3072,896]{1,0:T(8,128)(2,1)} %bitcast.1, f32[768,896]{1,0:T(8,128)} %fusion.17), kind=kOutput, calls=%fused_computation.5 | convolution fusion | flops 4236410880 | bytes 12976128 | tf_op jit(solution)/shard_map/dot_general | solution.py:12
  203.5 6.7 %copy.15 = bf16[768,3072]{0,1:T(8,128)(2,1)} copy(bf16[768,3072]{1,0:T(8,128)(2,1)} %convolution_convert_fusion.1) | data formatting | bytes 9437184
  210.1 0.0 copy-start.6
  210.1 0.0 copy-start.2
  210.1 0.0 reduce-scatter.10.cloned.1.call-update
  210.2 0.0 all-gather.11.cloned.1.call-start
  210.2 0.5 all-gather.11.cloned.1.call-update
  210.7 0.0 all-gather.9.cloned.1.call-start
  210.8 0.0 copy-done
  210.8 0.0 copy-done.6
  210.8 0.3 fusion.10
  211.1 0.1 mul.99
  211.2 54.5 %reduce-scatter.10.cloned.1.call-done = bf16[384,768]{1,0:T(8,128)(2,1)} async-done(((bf16[3072,768]{1,0:T(8,128)(2,1)}), bf16[384,768]{1,0:T(8,128)(2,1)}) %reduce-scatter.10.cloned.1.call-update) | async-done | bytes 589840
  265.7 1.4 copy.16
  267.1 0.0 copy-done.2
  267.1 0.0 copy-done.3
  267.1 1.1 fusion.11
  268.2 0.0 all-gather.9.cloned.1.call-update
  268.2 0.0 reduce-scatter.12.cloned.1.call-start
  268.3 60.0 %all-gather.11.cloned.1.call-done = bf16[3072,896]{1,0:T(8,128)(2,1)} async-done(((bf16[192,896]{1,0:T(8,128)(2,1)}), bf16[3072,896]{1,0:T(8,128)(2,1)}) %all-gather.11.cloned.1.call-update) | async-done | bytes 5505040 | tf_op jit(solution)/shard_map/all_gather | solution.py:64
  328.3 56.9 %all-gather.9.cloned.1.call-done = bf16[768,3072]{1,0:T(8,128)(2,1)} async-done(((bf16[768,384]{1,0:T(8,128)(2,1)}), bf16[768,3072]{1,0:T(8,128)(2,1)}) %all-gather.9.cloned.1.call-update) | async-done | bytes 4718608 | tf_op jit(solution)/shard_map/all_gather | solution.py:62
  385.2 10.0 %fusion.8 = bf16[768,896]{1,0:T(8,128)(2,1)S(1)} fusion(f32[768,896]{1,0:T(8,128)} %fusion.17, bf16[768,3072]{1,0:T(8,128)(2,1)} %all-gather.9.cloned.1.call-done, bf16[3072,896]{1,0:T(8,128)(2,1)} %all-gather.11.cloned.1.call-done), kind=kOutput, calls=%fused_computation.15 | convolution fusion | flops 4241620992 | bytes 14352384 | tf_op jit(solution)/shard_map/dot_general | solution.py:41
  395.2 0.0 copy-start.8
  395.2 1.1 copy-done.8
  396.3 9.3 %convolution_convert_fusion = bf16[768,3072]{1,0:T(8,128)(2,1)} fusion(bf16[768,896]{1,0:T(8,128)(2,1)S(1)} %fusion.8, bf16[3072,896]{1,0:T(8,128)(2,1)} %all-gather.7.cloned.1.call-done), kind=kOutput, calls=%fused_computation.4 | convolution fusion | flops 4230217728 | bytes 11599872 | tf_op jit(solution)/shard_map/dot_general | solution.py:12
  405.6 6.6 %copy.17 = bf16[768,3072]{0,1:T(8,128)(2,1)} copy(bf16[768,3072]{1,0:T(8,128)(2,1)} %convolution_convert_fusion) | data formatting | bytes 9437184
  412.2 0.0 reduce-scatter.12.cloned.1.call-update
  412.2 0.2 reduce-scatter.14.cloned.1.call-start
  412.5 0.0 copy-start.7
  412.5 6.9 %fusion.18 = f32[3072,896]{0,1:T(8,128)S(1)} fusion(bf16[768,3072]{1,0:T(8,128)(2,1)} %fusion.1, bf16[768,896]{1,0:T(8,128)(2,1)} %copy-done.8), kind=kOutput, calls=%fused_computation.32 | convolution fusion | flops 4227858432 | bytes 17104896 | tf_op jit(solution)/shard_map/dot_general | solution.py:74
  419.4 0.0 copy-done.7
  419.4 7.1 %fusion.15 = f32[3072,896]{0,1:T(8,128)S(1)} fusion(bf16[768,3072]{1,0:T(8,128)(2,1)} %all-gather.9.cloned.1.call-done, f32[768,896]{1,0:T(8,128)S(1)} %copy-done.7), kind=kOutput, calls=%fused_computation.29 | convolution fusion | flops 4234051584 | bytes 18481152 | tf_op jit(solution)/shard_map/dot_general | solution.py:77
  426.5 6.3 %fusion = bf16[3072,1792]{0,1:T(8,128)(2,1)} fusion(f32[3072,896]{0,1:T(8,128)S(1)} %fusion.15, f32[3072,896]{0,1:T(8,128)S(1)} %fusion.18), kind=kLoop, calls=%fused_computation.1 | loop fusion | flops 16515072 | bytes 33030144 | tf_op jit(solution)/shard_map/convert_element_type | solution.py:81
  432.9 14.0 %copy.19 = bf16[3072,1792]{1,0:T(8,128)(2,1)} copy(bf16[3072,1792]{0,1:T(8,128)(2,1)} %fusion) | data formatting | bytes 22020096
  446.9 0.0 reduce-scatter.14.cloned.1.call-update
  446.9 0.2 convolution_add_fusion.1
  447.1 22.1 %reduce-scatter.12.cloned.1.call-done = bf16[384,768]{1,0:T(8,128)(2,1)} async-done(((bf16[3072,768]{1,0:T(8,128)(2,1)}), bf16[384,768]{1,0:T(8,128)(2,1)}) %reduce-scatter.12.cloned.1.call-update) | async-done | bytes 589840
  469.2 1.4 copy.18
  470.6 1.4 fusion.9
  472.0 114.4 %reduce-scatter.14.cloned.1.call-done = bf16[192,1792]{1,0:T(8,128)(2,1)} async-done(((bf16[3072,1792]{1,0:T(8,128)(2,1)}), bf16[192,1792]{1,0:T(8,128)(2,1)}) %reduce-scatter.14.cloned.1.call-update) | async-done | bytes 688144
  586.4 1.4 copy.20
  587.8 0.1 fusion.16
  588.0 1.1 copy.14
  589.1 1.1 copy.13
  590.3 0.0 copy-done.1
  (3 shorter events, 0.0 us)
Async XLA Ops:
  7.2 203.6 %copy-start = (f32[32,16]{0,1:T(8,128)S(1)}, f32[32,16]{0,1:T(8,128)}, u32[]{:S(2)}) copy-start(f32[32,16]{0,1:T(8,128)} %param.11) | copy-start | bytes 6148
  7.2 147.7 %all-gather.5.cloned.1.call-start = ((), (), s32[]{:S(2)}) async-start(), calls=%async_computation.4 | async-start | bytes 5308416 | tf_op jit(solution)/shard_map/all_gather | solution.py:19
  7.9 176.3 %all-gather.7.cloned.1.call-start = ((), (), s32[]{:S(2)}) async-start(), calls=%async_computation.5 | async-start | bytes 5849088 | tf_op jit(solution)/shard_map/all_gather | solution.py:46
  12.8 9.5 %copy-start.4 = (bf16[32,384]{1,0:T(8,128)(2,1)S(1)}, bf16[32,384]{1,0:T(8,128)(2,1)}, u32[]{:S(2)}) copy-start(bf16[32,384]{1,0:T(8,128)(2,1)} %param.10) | copy-start | bytes 73732
  12.8 141.9 %copy-start.5 = (s32[3]{0:T(128)S(1)}, s32[3]{0:T(128)}, u32[]{:S(2)}) copy-start(s32[3]{0:T(128)} %param.14) | copy-start | bytes 40
  12.8 181.1 %all-to-all-start = ((bf16[16,192,896]{2,1,0:T(8,128)(2,1)}), bf16[16,192,896]{2,1,0:T(8,128)(2,1)}, u32[]{:S(2)}, u32[]{:S(2)}) async-start(bf16[16,192,896]{2,1,0:T(8,128)(2,1)} %stack.2), calls=%async_computation | async-start | bytes 11010048 | tf_op jit(solution)/shard_map/all_to_all | solution.py:51
  22.2 243.6 %reduce-scatter.10.cloned.1.call-start = ((), (), s32[]{:S(2)}) async-start(), calls=%async_computation.8 | async-start | bytes 5308416
  210.1 0.7 copy-start.6
  210.1 57.0 %copy-start.2 = (bf16[768,384]{1,0:T(8,128)(2,1)S(1)}, bf16[768,384]{1,0:T(8,128)(2,1)}, u32[]{:S(2)}) copy-start(bf16[768,384]{1,0:T(8,128)(2,1)} %param.8) | copy-start | bytes 1769476
  210.1 57.0 %copy-start.3 = (bf16[768,384]{1,0:T(8,128)(2,1)S(1)}, bf16[768,384]{1,0:T(8,128)(2,1)}, u32[]{:S(2)}) copy-start(bf16[768,384]{1,0:T(8,128)(2,1)} %param.9) | copy-start | bytes 1769476
  210.2 118.1 %all-gather.11.cloned.1.call-start = ((), (), s32[]{:S(2)}) async-start(), calls=%async_computation.7 | async-start | bytes 5849088 | tf_op jit(solution)/shard_map/all_gather | solution.py:64
  210.7 174.5 %all-gather.9.cloned.1.call-start = ((), (), s32[]{:S(2)}) async-start(), calls=%async_computation.6 | async-start | bytes 5308416 | tf_op jit(solution)/shard_map/all_gather | solution.py:62
  268.2 201.0 %reduce-scatter.12.cloned.1.call-start = ((), (), s32[]{:S(2)}) async-start(), calls=%async_computation.9 | async-start | bytes 5308416
  395.2 1.1 copy-start.8
  412.2 174.2 %reduce-scatter.14.cloned.1.call-start = ((), (), s32[]{:S(2)}) async-start(), calls=%async_computation.10 | async-start | bytes 11698176
  412.5 7.0 %copy-start.7 = (f32[768,896]{1,0:T(8,128)S(1)}, f32[768,896]{1,0:T(8,128)}, u32[]{:S(2)}) copy-start(f32[768,896]{1,0:T(8,128)} %fusion.17) | copy-start | bytes 8257540
  586.4 3.9 copy-start.1
Sparse Core Ops, SparseCore 0:
  9.7 104.5 all-gather.4
  116.7 67.4 all-gather.6
  210.3 55.4 reduce-scatter.9
  268.1 60.1 all-gather.10
  330.4 54.8 all-gather.8
  412.4 56.8 reduce-scatter.11
  473.6 112.7 reduce-scatter.13
